TPU v7x, 32 devices: a whole 2x2x4 slice. The times are simulated.
32 devices in a mesh: row: 8 (over z, y), col: 4 (over x, core).
Axes of the slice: x: 2, y: 2, z: 4, core: 2. Of those that a mesh axis runs over, the one named last changes fastest.
Arguments:
- a_weights: bfloat16 [4096, 1024], P('row', 'col'), may hold values from 0.0001 to 1, as said below
- tile_mask: int32 [8, 2], replicated, may hold values from 0 to 1, as said below
- pair_mask: int32 [8, 8], replicated, may hold values from 0 to 1, as said below
Outputs:
- jaccard: bfloat16 [4096, 4096], P('row', 'col')
Inputs may be any that keep to these rules, and one draw needn't show every extreme that they name: `a_weights`: all weights positive. `tile_mask`: 1 where a tile is present; tile (I, I mod 2) of every block row I is present. `pair_mask`: symmetric, with ones on the diagonal.
All inputs are finite; a program needn't handle non-finite values.
Results may differ from a plain program's by a relative error of at most 0.001.
Values may be sent and summed in bfloat16 or wider, within the bound.
A program may use at most 64 MiB of HBM per device.

v0:
```python
import jax
import jax.numpy as jnp
from jax import lax
from jax.sharding import PartitionSpec as P

BLOCK = 512


def broadcast(value, axis, source):
    kept = jnp.where(lax.axis_index(axis) == source, value, 0).astype(value.dtype)
    return lax.psum(kept, axis)


def expand_tiles(flags):
    return jnp.repeat(jnp.repeat(flags, BLOCK, axis=0), BLOCK, axis=1)


def body(a_weights, tile_mask, pair_mask):
    row_index = lax.axis_index("row")
    col_index = lax.axis_index("col")
    pair_count = lax.axis_size("row") // lax.axis_size("col")
    blocks_here = a_weights.shape[0] // BLOCK
    own_flags = lax.dynamic_slice_in_dim(tile_mask, row_index * blocks_here, blocks_here, 0)
    own_mask = expand_tiles(own_flags).astype(jnp.bfloat16)
    gathered = lax.all_gather(a_weights, "col", axis=1, tiled=True)
    own_panel = gathered * own_mask
    row_degree = jnp.einsum("ik,ik->i", own_panel, own_panel, preferred_element_type=jnp.float32)
    remotes = [
        broadcast(own_panel, "row", pair_count * col_index + offset) for offset in range(pair_count)
    ]
    outputs = []
    for offset in range(pair_count):
        col_first = (pair_count * col_index + offset) * blocks_here
        remote = remotes[offset]
        pair_tiles = lax.dynamic_slice(
            pair_mask, (row_index * blocks_here, col_first), (blocks_here, blocks_here)
        )
        pair_open = expand_tiles(pair_tiles) > 0
        col_degree = jnp.einsum("ik,ik->i", remote, remote, preferred_element_type=jnp.float32)
        shared = lax.dot_general(
            own_panel, remote, (((1,), (1,)), ((), ())), preferred_element_type=jnp.float32
        )
        weights = shared / (row_degree[:, None] + col_degree[None, :] - shared)
        outputs.append(jnp.where(pair_open, weights, jnp.zeros_like(weights)))
    return jnp.concatenate(outputs, axis=1).astype(jnp.bfloat16)


def solution(mesh):
    in_specs = (P("row", "col"), P(), P())
    out_specs = P("row", "col")
    return jax.shard_map(body, mesh=mesh, in_specs=in_specs, out_specs=out_specs, check_vma=False)
```

profile of v0, /device:TPU:0, one launch (start us, length us, event | category | flops | bytes accessed | tf_op | source)
XLA Modules:
  0.0 146.8 jit_solution(6093091236768662315)
XLA Ops:
  6.5 0.0 all-gather.2.cloned.1.call-start
  6.5 0.7 all-gather.2.cloned.1.call-update
  7.3 0.0 all-reduce.3.cloned.1.call-start
  7.3 0.9 fusion.17
  8.2 0.1 broadcast_bitcast_fusion
  8.3 20.2 %all-gather.2.cloned.1.call-done = bf16[512,1024]{1,0:T(8,128)(2,1)} async-done(((bf16[512,256]{1,0:T(8,128)(2,1)}), bf16[512,1024]{1,0:T(8,128)(2,1)}) %all-gather.2.cloned.1.call-update) | async-done | bytes 1048592 | tf_op jit(solution)/shard_map/all_gather | solution.py:25
  28.5 2.7 %broadcast_select_fusion.1 = (bf16[512,1024]{1,0:T(8,128)(2,1)}, bf16[512,1024]{1,0:T(8,128)(2,1)}) fusion(pred[]{:T(512)S(6)} %eq.6, bf16[512,1024]{1,0:T(8,128)(2,1)} %all-gather.2.cloned.1.call-done, bf16[1024]{0:T(1024)(128)(2,1)S(1)} %bitcast.7, pred[]{:T(512)S(6)} %eq.7), kind=kLoop, calls=%fused_computation.14 | loop fusion | flops 1572864 | bytes 3147778 | tf_op jit(solution)/shard_map/jit(_where)/select_n | solution.py:10
  31.2 0.0 copy-start
  31.2 0.0 all-reduce.3.cloned.1.call-update
  31.2 1.5 fusion.18
  34.0 0.0 copy-done
  34.0 0.3 fusion.2
  34.3 100.0 %all-reduce.3.cloned.1.call-done = (bf16[512,1024]{1,0:T(8,128)(2,1)}, bf16[512,1024]{1,0:T(8,128)(2,1)}) async-done(((bf16[512,1024]{1,0:T(8,128)(2,1)}, bf16[512,1024]{1,0:T(8,128)(2,1)}), (bf16[512,1024]{1,0:T(8,128)(2,1)}, bf16[512,1024]{1,0:T(8,128)(2,1)})) %all-reduce.3.cloned.1.call-update) | async-done | bytes 2097168 | tf_op jit(solution)/shard_map/psum | solution.py:11
  134.4 0.0 copy-start.2
  134.4 2.1 %fusion = (f32[512]{0:T(512)S(1)}, f32[512]{0:T(512)S(1)}) fusion(bf16[512,1024]{1,0:T(8,128)(2,1)} %get-tuple-element.5, bf16[512,1024]{1,0:T(8,128)(2,1)} %get-tuple-element.6), kind=kLoop, calls=%fused_computation.1 | loop fusion | flops 3144704 | bytes 2101248 | tf_op jit(solution)/shard_map/ik,ik->i/dot_general | solution.py:39
  136.5 0.0 copy-done.2
  136.5 0.0 copy-start.1
  136.5 0.8 fusion.4
  137.3 0.4 copy-done.1
  137.7 0.8 fusion.6
  138.5 0.1 pad_maximum_fusion
  138.6 1.3 copy.4
  (1 shorter events, 0.0 us)
Async XLA Ops:
  6.5 21.9 %all-gather.2.cloned.1.call-start = ((), (), s32[]{:S(2)}) async-start(), calls=%async_computation | async-start | bytes 1310720 | tf_op jit(solution)/shard_map/all_gather | solution.py:25
  7.3 127.1 %all-reduce.3.cloned.1.call-start = ((), (), s32[]{:S(2)}) async-start(), calls=%async_computation.1 | async-start | bytes 4194304 | tf_op jit(solution)/shard_map/psum | solution.py:11
  31.2 2.8 %copy-start = (bf16[512,1024]{1,0:T(8,128)(2,1)S(1)}, bf16[512,1024]{1,0:T(8,128)(2,1)}, u32[]{:S(2)}) copy-start(bf16[512,1024]{1,0:T(8,128)(2,1)} %all-gather.2.cloned.1.call-done) | copy-start | bytes 3145732
  134.4 2.1 %copy-start.2 = (bf16[512,1024]{1,0:T(8,128)(2,1)S(1)}, bf16[512,1024]{1,0:T(8,128)(2,1)}, u32[]{:S(2)}) copy-start(bf16[512,1024]{1,0:T(8,128)(2,1)} %get-tuple-element.6) | copy-start | bytes 3145732
  136.5 1.2 copy-start.1
Sparse Core Ops, SparseCore 0:
  8.9 19.5 all-gather.1
  32.1 102.1 all-reduce.2
where the time goes:
time: 147 us
  waiting for transfers between devices  121 us (82%)
  between operations  14.8 us (10%)
  other arithmetic  6.09 us (4%)
  local copies, waits for them, and re-layouts  3.28 us (2%)
  matrix products  1.58 us (1%)
    psum x1, waiting for transfers between devices, broadcast(): return lax.psum(kept, axis)  100 us
    all_gather x1, waiting for transfers between devices, body(): gathered = lax.all_gather(a_weights, 'col', axis=1, tiled=True)  20.2 us
  transfers between devices with their start and end apart: 2, of which 2 were waited for; matrix products, arithmetic and copies ran while one was open for 2% of the time, Pallas kernels for 0%

commit v1 on v0

--- a/solution.py
+++ b/solution.py
@@ -8,7 +8,7 @@
 
 def broadcast(value, axis, source):
     kept = jnp.where(lax.axis_index(axis) == source, value, 0).astype(value.dtype)
-    return lax.psum(kept, axis)
+    return jnp.sum(lax.all_gather(kept, axis), axis=0)
 
 
 def expand_tiles(flags):

time: 147 us -> 297 us (2.02)
  waiting for transfers between devices: 121 us -> 262 us
  other arithmetic: 6.09 us -> 16 us
    all_gather x0 -> x2, waiting for transfers between devices: none -> 241 us  [broadcast(): return jnp.sum(lax.all_gather(kept, axis), axis=0)]
    psum x1 -> x0, waiting for transfers between devices: 100 us -> none  [broadcast(): return lax.psum(kept, axis)]
    reduce_sum x0 -> x2, other arithmetic: none -> 11.3 us  [broadcast(): return jnp.sum(lax.all_gather(kept, axis), axis=0)]
  transfers between devices with their start and end apart: 2 -> 3, of which waited for: 2 -> 3; matrix products, arithmetic and copies ran while one was open for 2% -> 3% of each run, Pallas kernels for 0% -> 0%
where the time goes in v1:
time: 297 us
  waiting for transfers between devices  262 us (88%)
  other arithmetic  16 us (5%)
  between operations  14.3 us (5%)
    all_gather x2, waiting for transfers between devices, broadcast(): return jnp.sum(lax.all_gather(kept, axis), axis=0)  241 us
    all_gather x1, waiting for transfers between devices, body(): gathered = lax.all_gather(a_weights, 'col', axis=1, tiled=True)  20.2 us
    reduce_sum x2, other arithmetic, broadcast(): return jnp.sum(lax.all_gather(kept, axis), axis=0)  11.3 us
  transfers between devices with their start and end apart: 3, of which 3 were waited for; matrix products, arithmetic and copies ran while one was open for 3% of the time, Pallas kernels for 0%

profile of v1, /device:TPU:0, one launch (start us, length us, event | category | flops | bytes accessed | tf_op | source)
XLA Modules:
  0.0 297.2 jit_solution(7134248792690212686)
XLA Ops:
  6.5 0.0 all-gather.6.cloned.1.call-start
  6.5 0.7 all-gather.6.cloned.1.call-update
  7.3 0.0 all-gather.8.cloned.1.call-start
  7.3 0.9 fusion.17
  8.2 0.1 broadcast_bitcast_fusion
  8.3 20.2 %all-gather.6.cloned.1.call-done = bf16[512,1024]{1,0:T(8,128)(2,1)} async-done(((bf16[512,256]{1,0:T(8,128)(2,1)}), bf16[512,1024]{1,0:T(8,128)(2,1)}) %all-gather.6.cloned.1.call-update) | async-done | bytes 1048592 | tf_op jit(solution)/shard_map/all_gather | solution.py:25
  28.5 0.0 copy-start
  28.5 2.8 broadcast_select_fusion.1
  31.3 0.0 all-gather.8.cloned.1.call-update
  31.3 0.0 all-gather.10.cloned.1.call-start
  31.3 0.7 all-gather.10.cloned.1.call-update
  32.0 1.4 fusion.18
  34.6 0.0 copy-done
  34.6 0.3 fusion.2
  34.9 121.5 %all-gather.8.cloned.1.call-done = bf16[4096,1024]{1,0:T(8,128)(2,1)} async-done(((bf16[512,1024]{1,0:T(8,128)(2,1)}), bf16[4096,1024]{1,0:T(8,128)(2,1)}) %all-gather.8.cloned.1.call-update) | async-done | bytes 8388624 | tf_op jit(solution)/shard_map/all_gather | solution.py:11
  156.4 5.7 %reduce_sum.24 = bf16[512,1024]{1,0:T(8,128)(2,1)S(1)} reduce(bf16[8,512,1024]{2,1,0:T(8,128)(2,1)} %bitcast.9, bf16[]{:T(256)} %constant.26.clone.1), dimensions={0}, to_apply=%region_0.1 | reduce | flops 3670016 | bytes 9437186 | tf_op jit(solution)/shard_map/reduce_sum | solution.py:11
  162.1 0.3 fusion.1
  162.3 119.3 %all-gather.10.cloned.1.call-done = bf16[4096,1024]{1,0:T(8,128)(2,1)} async-done(((bf16[512,1024]{1,0:T(8,128)(2,1)}), bf16[4096,1024]{1,0:T(8,128)(2,1)}) %all-gather.10.cloned.1.call-update) | async-done | bytes 8388624 | tf_op jit(solution)/shard_map/all_gather | solution.py:11
  281.7 5.7 %reduce_sum.25 = bf16[512,1024]{1,0:T(8,128)(2,1)S(1)} reduce(bf16[8,512,1024]{2,1,0:T(8,128)(2,1)} %bitcast.10, bf16[]{:T(256)} %constant.26.clone.1), dimensions={0}, to_apply=%region_1.2 | reduce | flops 3670016 | bytes 9437186 | tf_op jit(solution)/shard_map/reduce_sum | solution.py:11
  287.4 0.3 fusion
  287.6 0.8 fusion.4
  288.4 0.8 fusion.6
  289.2 0.1 pad_maximum_fusion
  289.3 1.3 copy.4
  (1 shorter events, 0.0 us)
Async XLA Ops:
  6.5 21.9 %all-gather.6.cloned.1.call-start = ((), (), s32[]{:S(2)}) async-start(), calls=%async_computation | async-start | bytes 1310720 | tf_op jit(solution)/shard_map/all_gather | solution.py:25
  7.3 149.1 %all-gather.8.cloned.1.call-start = ((), (), s32[]{:S(2)}) async-start(), calls=%async_computation.1 | async-start | bytes 9437184 | tf_op jit(solution)/shard_map/all_gather | solution.py:11
  28.5 6.1 %copy-start = (bf16[512,1024]{1,0:T(8,128)(2,1)S(1)}, bf16[512,1024]{1,0:T(8,128)(2,1)}, u32[]{:S(2)}) copy-start(bf16[512,1024]{1,0:T(8,128)(2,1)} %all-gather.6.cloned.1.call-done) | copy-start | bytes 3145732
  31.3 250.4 %all-gather.10.cloned.1.call-start = ((), (), s32[]{:S(2)}) async-start(), calls=%async_computation.2 | async-start | bytes 9437184 | tf_op jit(solution)/shard_map/all_gather | solution.py:11
Sparse Core Ops, SparseCore 0:
  8.9 19.5 all-gather.5
  31.4 124.9 all-gather.7
  158.5 123.1 all-gather.9

commit v2 on v0

--- a/solution.py
+++ b/solution.py
@@ -4,6 +4,28 @@
 from jax.sharding import PartitionSpec as P
 
 BLOCK = 512
+
+
+def laid_out(pieces, dim):
+    lengths = list(pieces.shape[1:])
+    lengths[dim] *= pieces.shape[0]
+    return jnp.moveaxis(pieces, 0, dim).reshape(lengths)
+
+
+def ring_gather(value, axis, dim):
+    size = lax.axis_size(axis)
+    pairs = [(i, (i + 1) % size) for i in range(size)]
+    back = [(b, a) for a, b in pairs]
+    lower, upper = ([], [])
+    for hop in range(size - 1):
+        if hop % 2 == 0:
+            lower.append(lax.ppermute(lower[-1] if lower else value, axis, pairs))
+        else:
+            upper.append(lax.ppermute(upper[-1] if upper else value, axis, back))
+    blocks = jnp.stack([*lower[::-1], value, *upper])
+    shift = lax.axis_index(axis) - len(lower)
+    blocks = blocks[(jnp.arange(size) - shift) % size]
+    return laid_out(blocks, dim)
 
 
 def broadcast(value, axis, source):
@@ -22,7 +44,7 @@
     blocks_here = a_weights.shape[0] // BLOCK
     own_flags = lax.dynamic_slice_in_dim(tile_mask, row_index * blocks_here, blocks_here, 0)
     own_mask = expand_tiles(own_flags).astype(jnp.bfloat16)
-    gathered = lax.all_gather(a_weights, "col", axis=1, tiled=True)
+    gathered = ring_gather(a_weights, "col", 1)
     own_panel = gathered * own_mask
     row_degree = jnp.einsum("ik,ik->i", own_panel, own_panel, preferred_element_type=jnp.float32)
     remotes = [

time: 147 us -> 142 us (0.966)
  waiting for transfers between devices: 121 us -> 110 us
  starting transfers between devices: 0.04 us -> 5.07 us
  other arithmetic: 6.09 us -> 4.35 us
  matrix products: 1.58 us -> 3.09 us
    all_gather x1 -> x0, waiting for transfers between devices: 20.2 us -> none  [body(): gathered = lax.all_gather(a_weights, 'col', axis=1, tiled=True)]
    ppermute x0 -> x3, waiting for transfers between devices: none -> 6.54 us  [the longest x2 6.53 us: ring_gather(): lower.append(lax.ppermute(lower[-1] if lower else value, axis, pairs))]
    ppermute x0 -> x3, starting transfers between devices: none -> 5.07 us  [the longest x2 3.14 us: ring_gather(): lower.append(lax.ppermute(lower[-1] if lower else value, axis, pairs))]
    psum x1, waiting for transfers between devices: 100 us -> 104 us  [broadcast(): return lax.psum(kept, axis)]
    dot_general x1, other arithmetic: 2.11 us -> 0.44 us  [body(): jnp.einsum('ik,ik->i', remote, remote, preferred_element_type=jnp.float32)]
    dot_general x2, matrix products: 1.58 us -> 3.09 us  [body(): lax.dot_general(own_panel, remote, (((1,), (1,)), ((), ())), preferred_el...]
  transfers between devices with their start and end apart: 2 -> 4, of which waited for: 2 -> 3; matrix products, arithmetic and copies ran while one was open for 2% -> 2% of each run, Pallas kernels for 0% -> 0%
where the time goes in v2:
time: 142 us; the launch traced here: 141 us
  waiting for transfers between devices  110 us (77%)
  between operations  14.7 us (10%)
  starting transfers between devices  5.07 us (4%)
  other arithmetic  4.35 us (3%)
  local copies, waits for them, and re-layouts  4 us (3%)
  matrix products  3.09 us (2%)
    psum x1, waiting for transfers between devices, broadcast(): return lax.psum(kept, axis)  104 us
    ppermute x2, waiting for transfers between devices, ring_gather(): lower.append(lax.ppermute(lower[-1] if lower else value, axis, pairs))  6.53 us
    ppermute x2, starting transfers between devices, ring_gather(): lower.append(lax.ppermute(lower[-1] if lower else value, axis, pairs))  3.14 us
    dot_general x2, matrix products, body(): lax.dot_general(own_panel, remote, (((1,), (1,)), ((), ())), preferred_el...  3.09 us
  transfers between devices with their start and end apart: 4, of which 3 were waited for; matrix products, arithmetic and copies ran while one was open for 2% of the time, Pallas kernels for 0%

profile of v2, /device:TPU:0, one launch (start us, length us, event | category | flops | bytes accessed | tf_op | source)
XLA Modules:
  0.0 141.4 jit_solution(16317404627656041968)
XLA Ops:
  6.5 0.0 all-reduce.3.cloned.1.call-start
  6.5 0.5 collective-permute-start
  7.0 1.9 %collective-permute-start.2 = (bf16[512,256]{1,0:T(8,128)(2,1)}, bf16[512,256]{1,0:T(8,128)(2,1)S(1)}, u32[]{:S(2)}, u32[]{:S(2)}) collective-permute-start(bf16[512,256]{1,0:T(8,128)(2,1)} %param.3), channel_id=1, source_target_pairs={{1,0},{2,1},{3,2},{0,3},{5,4},{6,5},{7,6},{4,7},{9,8},{10,9},{11,1... | collective-permute-start | bytes 786440 | tf_op jit(solution)/shard_map/ppermute | solution.py:24
  8.9 0.9 fusion.7
  9.8 3.5 %collective-permute-done = bf16[512,256]{1,0:T(8,128)(2,1)S(1)} collective-permute-done((bf16[512,256]{1,0:T(8,128)(2,1)}, bf16[512,256]{1,0:T(8,128)(2,1)S(1)}, u32[]{:S(2)}, u32[]{:S(2)}) %collective-permute-start) | collective-permute-done | bytes 262176 | tf_op jit(solution)/shard_map/ppermute | solution.py:22
  13.3 2.7 %collective-permute-start.1 = (bf16[512,256]{1,0:T(8,128)(2,1)S(1)}, bf16[512,256]{1,0:T(8,128)(2,1)S(1)}, u32[]{:S(2)}, u32[]{:S(2)}) collective-permute-start(bf16[512,256]{1,0:T(8,128)(2,1)S(1)} %collective-permute-done), channel_id=1, source_target_pairs={{0,1},{1,2},{2,3},{3,0},{4,5},{5,6},{6,7},{7,4},{8,9},{9,10},{10,1... | collective-permute-start | bytes 786440 | tf_op jit(solution)/shard_map/ppermute | solution.py:22
  16.0 0.1 broadcast_bitcast_fusion
  16.1 0.0 collective-permute-done.2
  16.1 3.0 %collective-permute-done.1 = bf16[512,256]{1,0:T(8,128)(2,1)S(1)} collective-permute-done((bf16[512,256]{1,0:T(8,128)(2,1)S(1)}, bf16[512,256]{1,0:T(8,128)(2,1)S(1)}, u32[]{:S(2)}, u32[]{:S(2)}) %collective-permute-start.1) | collective-permute-done | bytes 262176 | tf_op jit(solution)/shard_map/ppermute | solution.py:22
  19.1 1.1 pad_maximum_fusion
  20.2 0.6 gather_fusion
  20.8 0.5 copy.6
  21.4 0.4 fusion.2
  21.8 1.5 %broadcast_select_fusion.1 = (bf16[512,1024]{0,1:T(8,128)(2,1)}, bf16[512,1024]{0,1:T(8,128)(2,1)}) fusion(bf16[512,1024]{0,1:T(8,128)(2,1)S(1)} %get-tuple-element.8, pred[]{:T(512)S(6)} %eq.8, pred[]{:T(512)S(6)} %eq.9), kind=kLoop, calls=%fused_computation.17 | loop fusion | flops 1048576 | bytes 3145730 | tf_op jit(solution)/shard_map/jit(_where)/select_n | solution.py:32
  23.3 0.0 all-reduce.3.cloned.1.call-update
  23.3 1.4 %fusion.10 = (s32[1,1]{1,0:T(1,128)}, s32[1,1]{1,0:T(1,128)}) fusion(s32[8,8]{1,0:T(8,128)} %param.5, s32[]{:T(128)S(6)} %select_n.56, s32[]{:T(128)S(6)} %select_n.57, s32[]{:T(128)S(6)} %select_n.63), kind=kLoop, calls=%fused_computation.28 | loop fusion | bytes 28 | tf_op jit(solution)/shard_map/dynamic_slice | solution.py:57
  26.0 103.5 %all-reduce.3.cloned.1.call-done = (bf16[512,1024]{0,1:T(8,128)(2,1)}, bf16[512,1024]{0,1:T(8,128)(2,1)}) async-done(((bf16[512,1024]{0,1:T(8,128)(2,1)}, bf16[512,1024]{0,1:T(8,128)(2,1)}), (bf16[512,1024]{0,1:T(8,128)(2,1)}, bf16[512,1024]{0,1:T(8,128)(2,1)})) %all-reduce.3.cloned.1.call-update) | async-done | bytes 2097168 | tf_op jit(solution)/shard_map/psum | solution.py:33
  129.5 0.0 copy-start
  129.5 0.0 copy-start.1
  129.5 2.1 %fusion.11 = f32[512,512]{0,1:T(8,128)S(1)} fusion(bf16[512,1024]{0,1:T(8,128)(2,1)S(1)} %get-tuple-element.8, bf16[512,1024]{0,1:T(8,128)(2,1)} %get-tuple-element.5), kind=kOutput, calls=%fused_computation.29 | convolution fusion | flops 536870912 | bytes 3145728 | tf_op jit(solution)/shard_map/dot_general | solution.py:62
  131.7 0.0 copy-done
  131.7 0.0 copy-done.1
  131.7 0.4 fusion
  132.1 1.0 fusion.4
  133.1 0.1 pad_maximum_fusion.1
  133.2 1.3 copy.7
  (3 shorter events, 0.0 us)
Async XLA Ops:
  6.5 123.0 %all-reduce.3.cloned.1.call-start = ((), (), s32[]{:S(2)}) async-start(), calls=%async_computation | async-start | bytes 4194304 | tf_op jit(solution)/shard_map/psum | solution.py:33
  6.5 6.8 %collective-permute-start = (bf16[512,256]{1,0:T(8,128)(2,1)}, bf16[512,256]{1,0:T(8,128)(2,1)S(1)}, u32[]{:S(2)}, u32[]{:S(2)}) collective-permute-start(bf16[512,256]{1,0:T(8,128)(2,1)} %param.3), channel_id=1, source_target_pairs={{0,1},{1,2},{2,3},{3,0},{4,5},{5,6},{6,7},{7,4},{8,9},{9,10},{10,1... | collective-permute-start | bytes 786440 | tf_op jit(solution)/shard_map/ppermute | solution.py:22
  7.0 9.1 %collective-permute-start.2 = (bf16[512,256]{1,0:T(8,128)(2,1)}, bf16[512,256]{1,0:T(8,128)(2,1)S(1)}, u32[]{:S(2)}, u32[]{:S(2)}) collective-permute-start(bf16[512,256]{1,0:T(8,128)(2,1)} %param.3), channel_id=1, source_target_pairs={{1,0},{2,1},{3,2},{0,3},{5,4},{6,5},{7,6},{4,7},{9,8},{10,9},{11,1... | collective-permute-start | bytes 786440 | tf_op jit(solution)/shard_map/ppermute | solution.py:24
  13.3 5.8 %collective-permute-start.1 = (bf16[512,256]{1,0:T(8,128)(2,1)S(1)}, bf16[512,256]{1,0:T(8,128)(2,1)S(1)}, u32[]{:S(2)}, u32[]{:S(2)}) collective-permute-start(bf16[512,256]{1,0:T(8,128)(2,1)S(1)} %collective-permute-done), channel_id=1, source_target_pairs={{0,1},{1,2},{2,3},{3,0},{4,5},{5,6},{6,7},{7,4},{8,9},{9,10},{10,1... | collective-permute-start | bytes 786440 | tf_op jit(solution)/shard_map/ppermute | solution.py:22
  129.5 2.1 %copy-start = (bf16[512,1024]{0,1:T(8,128)(2,1)S(1)}, bf16[512,1024]{0,1:T(8,128)(2,1)}, u32[]{:S(2)}) copy-start(bf16[512,1024]{0,1:T(8,128)(2,1)} %get-tuple-element.6) | copy-start | bytes 3145732
  129.5 2.1 %copy-start.1 = (bf16[512,1024]{0,1:T(8,128)(2,1)S(1)}, bf16[512,1024]{0,1:T(8,128)(2,1)}, u32[]{:S(2)}) copy-start(bf16[512,1024]{0,1:T(8,128)(2,1)} %get-tuple-element.5) | copy-start | bytes 3145732
Sparse Core Ops, SparseCore 0:
  23.4 106.0 all-reduce.2
